TPU v7x, 32 devices: a whole 2x2x4 slice. The times are simulated.
32 devices in a mesh: expert: 16 (over z, x, core), tensor: 2 (over y).
Axes of the slice: x: 2, y: 2, z: 4, core: 2. Of those that a mesh axis runs over, the one named last changes fastest.
Arguments:
- tokens: bfloat16 [384, 4096], P('expert', 'tensor'), may hold values from -6 to 6
- grad_out: bfloat16 [384, 4096], P('expert', 'tensor'), may hold values from -6 to 6
- routing: int32 [384, 8], P('expert'), may hold values from 0 to 15, all different within a row; in each aligned block of 24 rows (0 to 23, 24 to 47, ...) at most 24 rows name the same one
- gates: float32 [384, 8], P('expert'), may hold values from 0.1 to 1
- w_in: bfloat16 [16, 4096, 2, 1536], P('expert', None, None, 'tensor'), may hold values from -0.09375 to 0.09375
- w_out: bfloat16 [16, 1536, 4096], P('expert', 'tensor'), may hold values from -0.15625 to 0.15625
Outputs:
- mixed: bfloat16 [384, 4096], P('expert', 'tensor')
- grad_tokens: bfloat16 [384, 4096], P('expert', 'tensor')
- grad_w_out: bfloat16 [16, 1536, 4096], P('expert', 'tensor')
Inputs may be any that keep to these rules, and one draw needn't show every extreme that they name: `routing`: each row names 8 different experts. Within each group of 24 tokens (the tokens held by one position of the `expert` axis (one token group)) no expert is named by more than 24 tokens, and some group names some expert exactly 24 times.
All inputs are finite; a program needn't handle non-finite values.
Results may differ from a plain program's by a relative error of at most 0.015.
Values may be sent and summed in bfloat16 or wider, within the bound.
A program may use at most 128 MiB of HBM per device.

v0:
```python
import functools

import jax
import jax.numpy as jnp
from jax import lax
from jax.experimental import pallas as pl
from jax.experimental.pallas import tpu as pltpu
from jax.sharding import PartitionSpec as P


def dispatched(tokens, grad_out, routing, gates, w_in, w_out):
    n_experts = lax.axis_size("expert")
    tok_rows = tokens.shape[0]
    topk_count = routing.shape[1]
    slot_cap = min(tok_rows, 16 * tok_rows // n_experts)
    slot_rows = n_experts * slot_cap
    model_width = w_out.shape[2]
    hidden = w_out.shape[1]
    experts = jnp.arange(n_experts, dtype=jnp.int32)
    is_named = (routing[:, :, None] == experts).astype(jnp.int32)
    counts = jnp.sum(is_named, axis=1)
    before = jnp.cumsum(counts, axis=0) - counts
    slot_index = jnp.sum(is_named * before[:, None, :], axis=2)
    target = (routing * slot_cap + slot_index).reshape(-1)
    placing = (jnp.arange(slot_rows, dtype=jnp.int32)[:, None] == target[None, :]).astype(
        jnp.bfloat16
    )
    scaled = (gates[:, :, None] * grad_out[:, None, :].astype(jnp.float32)).astype(jnp.bfloat16)
    scaled = scaled.reshape(tok_rows * topk_count, -1)
    sent_dy = jnp.dot(placing, scaled, preferred_element_type=jnp.float32).astype(jnp.bfloat16)
    w_both = w_in[0].reshape(model_width, 2 * hidden)
    w_down = w_out[0]
    contract_last = (((1,), (1,)), ((), ()))
    contract_first = (((0,), (0,)), ((), ()))
    whole = lax.all_gather(tokens, "tensor", axis=1, tiled=True)
    x_copies = jnp.repeat(whole, topk_count, axis=0)
    sent_x = jnp.dot(placing, x_copies, preferred_element_type=jnp.float32).astype(jnp.bfloat16)
    recv_x, recv_dy = (
        lax.all_to_all(sent_x, "expert", split_axis=0, concat_axis=0, tiled=True),
        lax.all_to_all(sent_dy, "expert", split_axis=0, concat_axis=0, tiled=True),
    )
    gate_up = jnp.dot(recv_x, w_both, preferred_element_type=jnp.float32)
    dy_piece = lax.all_gather(recv_dy, "tensor", axis=1, tiled=True)
    act_grad = lax.dot_general(dy_piece, w_down, contract_last, preferred_element_type=jnp.float32)
    dy_full = dy_piece
    act_grad, dy_full = (act_grad, dy_full)
    gate_proj = gate_up[:, :hidden]
    up_proj = gate_up[:, hidden:]
    sig_gate = jax.nn.sigmoid(gate_proj)
    activation = (gate_proj * sig_gate * up_proj).astype(jnp.bfloat16)
    grad_gate = act_grad * up_proj * sig_gate * (1.0 + gate_proj * (1.0 - sig_gate))
    grad_up = act_grad * gate_proj * sig_gate
    grad_both = jnp.concatenate([grad_gate, grad_up], axis=1).astype(jnp.bfloat16)
    out_part = jnp.dot(activation, w_down, preferred_element_type=jnp.float32)
    in_part = lax.dot_general(grad_both, w_both, contract_last, preferred_element_type=jnp.float32)
    grad_down = lax.dot_general(
        activation, dy_full, contract_first, preferred_element_type=jnp.float32
    )
    grad_down = grad_down.astype(jnp.bfloat16)[None]
    out_sum, in_sum = (
        lax.psum_scatter(
            out_part.astype(jnp.bfloat16), "tensor", scatter_dimension=1, tiled=True
        ).astype(jnp.float32),
        lax.psum_scatter(
            in_part.astype(jnp.bfloat16), "tensor", scatter_dimension=1, tiled=True
        ).astype(jnp.float32),
    )
    back_out, back_in = (
        lax.all_to_all(
            out_sum.astype(jnp.bfloat16), "expert", split_axis=0, concat_axis=0, tiled=True
        ).astype(out_sum.dtype),
        lax.all_to_all(
            in_sum.astype(jnp.bfloat16), "expert", split_axis=0, concat_axis=0, tiled=True
        ).astype(in_sum.dtype),
    )
    place_wide = placing.astype(jnp.float32)
    picked_out = lax.dot_general(
        place_wide,
        back_out,
        contract_first,
        precision=lax.Precision.HIGHEST,
        preferred_element_type=jnp.float32,
    )
    picked_in = lax.dot_general(
        place_wide,
        back_in,
        contract_first,
        precision=lax.Precision.HIGHEST,
        preferred_element_type=jnp.float32,
    )
    picked_out = picked_out.reshape(tok_rows, topk_count, -1)
    picked_in = picked_in.reshape(tok_rows, topk_count, -1)
    mixed = jnp.sum(gates[:, :, None] * picked_out, axis=1).astype(jnp.bfloat16)
    grad_tokens = jnp.sum(picked_in, axis=1).astype(jnp.bfloat16)
    return (mixed, grad_tokens, grad_down)

MESH = pl.DeviceIdType.MESH
F32 = jnp.float32
BF16 = jnp.bfloat16
NT = (((1,), (1,)), ((), ()))


def fused_kernel(
    n_z,
    tok_ref,
    dy_ref,
    routing_ref,
    gates_ref,
    w_in_hbm,
    w_out_hbm,
    mixed_ref,
    gtok_ref,
    act_t_hbm,
    scaled_hbm,
    tables,
    gate_ref,
    raw,
    buf,
    parts,
    sib_in,
    one_a,
    one_b,
    two,
    three,
    xs,
    scaled,
    gate_up,
    act_grad,
    act,
    act_t,
    grad_both,
    w_in,
    w_out,
    w_sem,
    raw_sem,
    tz_send,
    tx_send,
    ts_send,
    t_recv,
    gz_send,
    gx_send,
    gy_send,
    gs_send,
    g_recv,
    s_send,
    s_recv,
    one_send,
    one_a_recv,
    one_b_recv,
    two_send,
    two_recv,
    three_send,
    three_recv,
    out_sem,
):
    rows, width = tok_ref.shape
    part = width // 2
    n_chips = 2 * n_z
    hidden = w_out.shape[0]
    expert = lax.axis_index("expert")
    y = lax.axis_index("tensor")
    core = lax.rem(expert, 2)
    x = lax.rem(expert // 2, 2)
    z = expert // 4
    other = 1 - core

    def expert_at(j, dx, c):
        return lax.rem(z + j, n_z) * 4 + lax.rem(x + dx, 2) * 2 + c

    def chip_at(j, dx):
        return lax.rem(z + j, n_z) * 2 + lax.rem(x + dx, 2)

    def quarter(dy, h):
        return lax.rem(y + dy, 2) * 2 + h

    to_x = (expert_at(0, 1, core), y)
    to_y = (expert, 1 - y)
    to_sib = (expert_at(0, 0, other), y)

    def to_z(j):
        return (expert_at(j, 0, core), y)

    depth = raw.shape[1]
    n_loads = w_in_hbm.shape[0] // depth

    def load(i):
        return pltpu.make_async_copy(
            w_in_hbm.at[pl.ds(i * depth, depth)], raw.at[i % 2], raw_sem.at[i % 2]
        )

    load_out = pltpu.make_async_copy(w_out_hbm, w_out, w_sem.at[0])
    load(0).start()
    load(1).start()
    load_out.start()

    def split(i):
        load(i).wait()
        some = 64

        def step(k, carry):
            at = pl.ds(pl.multiple_of(k * some, some), some)
            to = pl.ds(pl.multiple_of(i * depth + k * some, some), some)
            w_in[to, :] = raw[i % 2, at].reshape(some, 2 * hidden)
            return carry

        lax.fori_loop(0, depth // some, step, 0)
        if i + 2 < n_loads:
            load(i + 2).start()

    barrier = pltpu.get_barrier_semaphore()
    partners = [to_z(j) for j in range(1, n_z)] + [to_x, to_y, to_sib]
    for partner in partners:
        pl.semaphore_signal(barrier, inc=1, device_id=partner, device_id_type=MESH)

    own = jnp.concatenate([tok_ref[...].astype(F32), dy_ref[...].astype(F32)], axis=0)
    for h in range(2):
        buf[expert, quarter(0, h)] = own[:, h * part : (h + 1) * part].astype(BF16)
    lanes_of = lax.broadcasted_iota(jnp.int32, (rows, 128), 1)
    named, weight = routing_ref[...], gates_ref[...]
    table = jnp.zeros((rows, 128), F32)
    for k in range(named.shape[1]):
        table += jnp.where(named[:, k : k + 1] == lanes_of, weight[:, k : k + 1], 0.0)
    tables[expert] = table
    pl.semaphore_wait(barrier, len(partners))

    pending = []

    def send(src, dst, send_sem, recv_sem, target):
        copy = pltpu.make_async_remote_copy(
            src_ref=src,
            dst_ref=dst,
            send_sem=send_sem,
            recv_sem=recv_sem,
            device_id=target,
            device_id_type=MESH,
        )
        copy.start()
        pending.append(copy)
        return copy

    def pass_on(j, dx, dy, h, target, sem):
        e, q = expert_at(j, dx, core), quarter(dy, h)
        send(buf.at[e, q], buf.at[e, q], sem, g_recv.at[e, q], target)

    def arrived(j, dx, dy, h, c):
        e, q = expert_at(j, dx, c), quarter(dy, h)
        pltpu.make_async_remote_copy(
            src_ref=buf.at[e, q],
            dst_ref=buf.at[e, q],
            send_sem=gs_send.at[0],
            recv_sem=g_recv.at[e, q],
            device_id=to_sib,
            device_id_type=MESH,
        ).wait_recv()

    def to_sibling(j, dx, dy, h):
        pass_on(j, dx, dy, h, to_sib, gs_send.at[((j * 2 + dx) * 2 + dy) * 2 + h])

    def along_x(j, dy, h):
        pass_on(j, 0, dy, h, to_x, gx_send.at[(j * 2 + dy) * 2 + h])

    def along_y(j, dx, h):
        pass_on(j, dx, 0, h, to_y, gy_send.at[(j * 2 + dx) * 2 + h])

    def pass_table(j, dx, target, sem):
        e = expert_at(j, dx, core)
        send(tables.at[e], tables.at[e], sem, t_recv.at[e], target)

    def table_arrived(j, dx, c):
        e = expert_at(j, dx, c)
        pltpu.make_async_remote_copy(
            src_ref=tables.at[e],
            dst_ref=tables.at[e],
            send_sem=ts_send.at[0],
            recv_sem=t_recv.at[e],
            device_id=to_sib,
            device_id_type=MESH,
        ).wait_recv()

    def spread(j, h):
        if j:
            arrived(j, 0, 0, h, core)
        along_x(j, 0, h)
        along_y(j, 0, h)
        to_sibling(j, 0, 0, h)

    def spread_table(j):
        if j:
            table_arrived(j, 0, core)
        pass_table(j, 0, to_x, tx_send.at[j])
        pass_table(j, 0, to_sib, ts_send.at[2 * j])

    def second_a(j):
        arrived(j, 1, 0, 0, core)
        along_y(j, 1, 0)
        to_sibling(j, 1, 0, 0)

    def second_b(j):
        arrived(j, 0, 1, 1, core)
        along_x(j, 1, 1)
        to_sibling(j, 0, 1, 1)

    z_order = [1, n_z - 1] + list(range(2, n_z - 1))
    near, rest = z_order[:2], z_order[2:]
    for j in z_order:
        pass_table(0, 0, to_z(j), tz_send.at[j - 1])
    for h in range(2):
        for j in z_order:
            pass_on(0, 0, 0, h, to_z(j), gz_send.at[(j - 1) * 2 + h])
    spread(0, 0)
    spread(0, 1)
    spread_table(0)
    per = -(-n_loads // 4)

    def split_some(k):
        for i in range(k * per, min((k + 1) * per, n_loads)):
            split(i)

    split_some(0)
    for j in near:
        spread_table(j)
        spread(j, 0)
    second_a(0)
    second_b(0)
    split_some(1)
    for j in rest:
        spread_table(j)
        spread(j, 0)
    for j in near:
        second_a(j)
    split_some(2)
    for j in near:
        spread(j, 1)
    for j in rest:
        second_a(j)
    split_some(3)
    for j in rest:
        spread(j, 1)
    for j in z_order:
        second_b(j)
    for j in range(n_z):
        table_arrived(j, 1, core)
        pass_table(j, 1, to_sib, ts_send.at[2 * j + 1])
    for j in range(n_z):
        for dx in range(2):
            table_arrived(j, dx, other)
    for e in range(2 * n_chips):
        mine = jnp.sum(jnp.where(lanes_of == expert, tables[e], 0.0), axis=1, keepdims=True)
        gate_ref[e * rows : (e + 1) * rows, :] = jnp.broadcast_to(mine, (rows, 128))

    keep_scaled = []

    def forward(dy, h, first):
        q = quarter(dy, h)

        def lay(p, carry):
            at = pl.ds(pl.multiple_of(p * (2 * rows), 2 * rows), 2 * rows)
            even = buf[2 * p, q].astype(F32)
            odd = buf[2 * p + 1, q].astype(F32)
            xs[at, :] = jnp.concatenate([even[:rows], odd[:rows]], axis=0).astype(BF16)
            both = jnp.concatenate([even[rows:], odd[rows:]], axis=0)
            scaled[q, at, :] = (gate_ref[at, 0:1] * both).astype(BF16)
            return carry

        lax.fori_loop(0, n_chips, lay, 0)
        k = len(keep_scaled)
        copy = pltpu.make_async_copy(scaled.at[q], scaled_hbm.at[q], out_sem.at[k])
        copy.start()
        keep_scaled.append(copy)
        if first:
            load_out.wait()
        tile = 256
        deep = pl.ds(pl.multiple_of(q * part, part), part)

        def gates_up(n, carry):
            at = pl.ds(pl.multiple_of(n * tile, tile), tile)
            piece = jnp.dot(xs[...], w_in[deep, at], preferred_element_type=F32)
            gate_up[:, at] = piece if first else gate_up[:, at] + piece
            return carry

        lax.fori_loop(0, 2 * hidden // tile, gates_up, 0)

        def grads(n, carry):
            at = pl.ds(pl.multiple_of(n * tile, tile), tile)
            piece = lax.dot_general(scaled[q], w_out[at, deep], NT, preferred_element_type=F32)
            act_grad[:, at] = piece if first else act_grad[:, at] + piece
            return carry

        lax.fori_loop(0, hidden // tile, grads, 0)

    def from_sibling(dy, h):
        for j in range(n_z):
            for dx in range(2):
                arrived(j, dx, dy, h, other)

    def third(dy, h, dxs):
        for j in [0] + z_order:
            for dx in dxs:
                arrived(j, dx, dy, h, core)
                to_sibling(j, dx, dy, h)

    from_sibling(0, 0)
    forward(0, 0, True)
    third(0, 1, [1])
    from_sibling(0, 1)
    forward(0, 1, False)
    third(1, 0, [0, 1])
    third(1, 1, [1])
    from_sibling(1, 0)
    forward(1, 0, False)
    from_sibling(1, 1)
    forward(1, 1, False)

    def middle(r, carry):
        at = pl.ds(pl.multiple_of(r * (2 * rows), 2 * rows), 2 * rows)
        gate_proj = gate_up[at, :hidden]
        up_proj = gate_up[at, hidden:]
        grad = act_grad[at, :]
        sig = jax.nn.sigmoid(gate_proj)
        act[at, :] = (gate_proj * sig * up_proj).astype(BF16)
        grad_both[at, :hidden] = (grad * up_proj * sig * (1.0 + gate_proj * (1.0 - sig))).astype(BF16)
        grad_both[at, hidden:] = (grad * gate_proj * sig).astype(BF16)
        return carry

    lax.fori_loop(0, n_chips, middle, 0)

    def backward(dy, h, part_at):
        q = quarter(dy, h)
        tile = 256
        steps = part // tile // 2

        def step(n, carry):
            lanes = pl.ds(pl.multiple_of(n * tile, tile), tile)
            at = pl.ds(pl.multiple_of(q * part + n * tile, tile), tile)
            out = jnp.dot(act[...], w_out[:, at], preferred_element_type=F32) * gate_ref[:, 0:1]
            back = lax.dot_general(grad_both[...], w_in[at, :], NT, preferred_element_type=F32)
            for e in range(2 * n_chips):
                take = slice(e * rows, (e + 1) * rows)
                parts[e % 2, q, e // 2, :, lanes] = jnp.concatenate(
                    [out[take], back[take]], axis=0
                ).astype(BF16)
            return carry

        lax.fori_loop(part_at * steps, (part_at + 1) * steps, step, 0)
        lanes = pl.ds(part_at * (part // 2), part // 2)
        sib_copies[dy, h, part_at] = send(
            parts.at[other, q, :, :, lanes],
            sib_in.at[q, :, :, lanes],
            s_send.at[q, part_at],
            s_recv.at[q, part_at],
            to_sib,
        )

    def chip_sum(dy, h):
        q = quarter(dy, h)
        sib_copies[dy, h, 0].wait_recv()
        sib_copies[dy, h, 1].wait_recv()

        def add(p, carry):
            parts[core, q, p] = (parts[core, q, p].astype(F32) + sib_in[q, p].astype(F32)).astype(BF16)
            return carry

        lax.fori_loop(0, n_chips, add, 0)

    def first_a(j, dx):
        p = chip_at(j, dx)
        return send(
            parts.at[core, quarter(1, 0), p],
            one_a.at[j * 2 + dx],
            one_send.at[j * 2 + dx],
            one_a_recv.at[j * 2 + dx],
            to_y,
        )

    def first_b(j, dy):
        k = j * 2 + dy
        return send(
            parts.at[core, quarter(dy, 1), chip_at(j, 1)],
            one_b.at[k],
            one_send.at[2 * n_z + k],
            one_b_recv.at[k],
            to_x,
        )

    far = [1 + k for k in range(n_z - 1)] + [0]
    a_copies, b_copies, sib_copies = {}, {}, {}
    backward(1, 0, 0)
    backward(1, 0, 1)
    backward(1, 1, 0)
    chip_sum(1, 0)
    for dx in (1, 0):
        for j in far:
            a_copies[j, dx] = first_a(j, dx)
    backward(1, 1, 1)
    backward(0, 1, 0)
    chip_sum(1, 1)
    for j in far:
        b_copies[j, 1] = first_b(j, 1)
    backward(0, 1, 1)
    backward(0, 0, 0)
    chip_sum(0, 1)
    for j in far:
        b_copies[j, 0] = first_b(j, 0)
    backward(0, 0, 1)
    chip_sum(0, 0)

    keep_act = pltpu.make_async_copy(act_t, act_t_hbm, w_sem.at[1])
    two_copies = {}
    for k, j in enumerate(far):
        if k == len(far) - 1:
            act_t[...] = act[...].T
            keep_act.start()
        p = chip_at(j, 1)
        qa, qb = quarter(0, 0), quarter(1, 1)
        a_copies[j, 1].wait_recv()
        parts[core, qa, p] = (
            parts[core, qa, p].astype(F32) + one_a[j * 2 + 1].astype(F32)
        ).astype(BF16)
        two_copies[j, 0] = send(
            parts.at[core, qa, p], two.at[0, j], two_send.at[0, j], two_recv.at[0, j], to_x
        )
        p = chip_at(j, 0)
        b_copies[j, 1].wait_recv()
        parts[core, qb, p] = (
            parts[core, qb, p].astype(F32) + one_b[j * 2 + 1].astype(F32)
        ).astype(BF16)
        two_copies[j, 1] = send(
            parts.at[core, qb, p], two.at[1, j], two_send.at[1, j], two_recv.at[1, j], to_y
        )

    three_copies = {}
    for j in far:
        for h in range(2):
            q, p = quarter(0, h), chip_at(j, 0)
            first = (a_copies, b_copies)[h]
            held = (one_a, one_b)[h]
            first[j, 0].wait_recv()
            two_copies[j, h].wait_recv()
            total = (
                parts[core, q, p].astype(F32)
                + held[j * 2].astype(F32)
                + two[h, j].astype(F32)
            )
            if j:
                parts[core, q, p] = total.astype(BF16)
                three_copies[j, h] = send(
                    parts.at[core, q, p],
                    three.at[h, j - 1],
                    three_send.at[h, j - 1],
                    three_recv.at[h, j - 1],
                    to_z(j),
                )
            else:
                for i in range(1, n_z):
                    three_copies[i, h].wait_recv()
                    total = total + three[h, i - 1].astype(F32)
                lanes = slice(h * part, (h + 1) * part)
                mixed_ref[:, lanes] = total[:rows].astype(BF16)
                gtok_ref[:, lanes] = total[rows:].astype(BF16)

    for copy in pending:
        copy.wait_send()
    for copy in keep_scaled:
        copy.wait()
    keep_act.wait()


def last_kernel(act_t_ref, scaled_ref, mixed_in, gtok_in, mixed_ref, gtok_ref, gdown_ref):
    @pl.when(pl.program_id(0) == 0)
    def _():
        mixed_ref[...] = mixed_in[...]
        gtok_ref[...] = gtok_in[...]

    gdown_ref[...] = jnp.dot(act_t_ref[...], scaled_ref[0], preferred_element_type=F32).astype(BF16)


def dense(tokens, grad_out, routing, gates, w_in, w_out):
    n_experts = lax.axis_size("expert")
    n_z = n_experts // 4
    rows, width = tokens.shape
    part = width // 2
    model_width, hidden = w_out.shape[2], w_out.shape[1]
    slots = n_experts * rows
    vmem = pl.BlockSpec(memory_space=pltpu.VMEM)
    anywhere = pl.BlockSpec(memory_space=pl.ANY)
    block = (2 * rows, part)
    dma = pltpu.SemaphoreType.DMA
    flops = 2 * slots * model_width * hidden * 7
    depth = max(model_width // 8, 64)
    mixed, gtok, act_t, scaled = pl.pallas_call(
        functools.partial(fused_kernel, n_z),
        out_shape=(
            jax.ShapeDtypeStruct((rows, width), BF16),
            jax.ShapeDtypeStruct((rows, width), BF16),
            jax.ShapeDtypeStruct((hidden, slots), BF16),
            jax.ShapeDtypeStruct((4, slots, part), BF16),
        ),
        in_specs=[vmem, vmem, vmem, vmem, anywhere, anywhere],
        out_specs=(vmem, vmem, anywhere, anywhere),
        scratch_shapes=[
            pltpu.VMEM((n_experts, rows, 128), F32),
            pltpu.VMEM((slots, 128), F32),
            pltpu.VMEM((2, depth, 2, hidden), BF16),
            pltpu.VMEM((n_experts, 4) + block, BF16),
            pltpu.VMEM((2, 4, 2 * n_z) + block, BF16),
            pltpu.VMEM((4, 2 * n_z) + block, BF16),
            pltpu.VMEM((2 * n_z,) + block, BF16),
            pltpu.VMEM((2 * n_z,) + block, BF16),
            pltpu.VMEM((2, n_z) + block, BF16),
            pltpu.VMEM((2, n_z - 1) + block, BF16),
            pltpu.VMEM((slots, part), BF16),
            pltpu.VMEM((4, slots, part), BF16),
            pltpu.VMEM((slots, 2 * hidden), F32),
            pltpu.VMEM((slots, hidden), F32),
            pltpu.VMEM((slots, hidden), BF16),
            pltpu.VMEM((hidden, slots), BF16),
            pltpu.VMEM((slots, 2 * hidden), BF16),
            pltpu.VMEM((model_width, 2 * hidden), BF16),
            pltpu.VMEM((hidden, model_width), BF16),
            dma((2,)),
            dma((2,)),
            dma((n_z - 1,)),
            dma((n_z,)),
            dma((2 * n_z,)),
            dma((n_experts,)),
            dma((2 * (n_z - 1),)),
            dma((4 * n_z,)),
            dma((4 * n_z,)),
            dma((8 * n_z,)),
            dma((n_experts, 4)),
            dma((4, 2)),
            dma((4, 2)),
            dma((4 * n_z,)),
            dma((2 * n_z,)),
            dma((2 * n_z,)),
            dma((2, n_z)),
            dma((2, n_z)),
            dma((2, n_z - 1)),
            dma((2, n_z - 1)),
            dma((4,)),
        ],
        compiler_params=pltpu.CompilerParams(
            collective_id=0, has_side_effects=True, vmem_limit_bytes=60 * 1024 * 1024
        ),
        cost_estimate=pl.CostEstimate(
            flops=flops, bytes_accessed=8 * model_width * hidden, transcendentals=slots * hidden
        ),
    )(tokens, grad_out, routing, gates, w_in[0], w_out[0])
    tile = part // 2
    whole = pl.BlockSpec((rows, width), lambda n: (0, 0))
    mixed, gtok, gdown = pl.pallas_call(
        last_kernel,
        grid=(8,),
        out_shape=(
            jax.ShapeDtypeStruct((rows, width), BF16),
            jax.ShapeDtypeStruct((rows, width), BF16),
            jax.ShapeDtypeStruct((hidden, model_width), BF16),
        ),
        in_specs=[
            pl.BlockSpec((hidden, slots), lambda n: (0, 0)),
            pl.BlockSpec((1, slots, tile), lambda n: (n // 2, 0, n % 2)),
            whole,
            whole,
        ],
        out_specs=(whole, whole, pl.BlockSpec((hidden, tile), lambda n: (0, n))),
        compiler_params=pltpu.CompilerParams(vmem_limit_bytes=32 * 1024 * 1024),
        cost_estimate=pl.CostEstimate(
            flops=flops // 7, bytes_accessed=4 * model_width * hidden, transcendentals=0
        ),
    )(act_t, scaled, mixed, gtok)
    return mixed, gtok, gdown[None]


def shards(tokens, grad_out, routing, gates, w_in, w_out):
    n_experts = lax.axis_size("expert")
    rows = tokens.shape[0]
    whole_groups = 16 * rows // n_experts >= rows
    if whole_groups and n_experts % 4 == 0 and n_experts >= 16 and lax.axis_size("tensor") == 2:
        return dense(tokens, grad_out, routing, gates, w_in, w_out)
    return dispatched(tokens, grad_out, routing, gates, w_in, w_out)


def solution(mesh):
    in_specs = (
        P("expert", "tensor"),
        P("expert", "tensor"),
        P("expert", None),
        P("expert", None),
        P("expert", None, None, "tensor"),
        P("expert", "tensor", None),
    )
    out_specs = (P("expert", "tensor"), P("expert", "tensor"), P("expert", "tensor", None))
    return jax.shard_map(shards, mesh=mesh, in_specs=in_specs, out_specs=out_specs, check_vma=False)
```

profile of v0, /device:TPU:9, one launch (start us, length us, event | category | flops | bytes accessed | tf_op | source)
XLA Modules:
  0.0 121.3 jit_solution(2662323086464958051)
XLA Ops:
  0.6 1.4 %copy.9.routing_ref = s32[24,8]{1,0:T(8,128)} copy(s32[24,8]{0,1:T(8,128)} %param.8) | data formatting | bytes 1536 | tf_op args[2]
  2.0 1.4 %copy.10.gates_ref = f32[24,8]{1,0:T(8,128)} copy(f32[24,8]{0,1:T(8,128)} %param.9) | data formatting | bytes 1536 | tf_op args[3]
  3.3 106.6 %shard_map.85 = (bf16[24,2048]{1,0:T(8,128)(2,1)}, bf16[24,2048]{1,0:T(8,128)(2,1)}, bf16[768,384]{1,0:T(8,128)(2,1)}, bf16[4,384,1024]{2,1,0:T(8,128)(2,1)}) custom-call(bf16[24,2048]{1,0:T(8,128)(2,1)} %tok_ref.1, bf16[24,2048]{1,0:T(8,128)(2,1)} %dy_ref.1, s32[24,8]{1,0:T(8,128)} %copy.9.routing_ref, f32[24,8]{1,0:T(8,128)} %copy.10.gates_ref, ...), custom_call_target="tpu_custom_call" | custom-call | flops 16911433728 | bytes 25165824 | tf_op jit(solution)/shard_map/pallas_call | solution.py:590
  110.0 0.0 copy-start
  110.0 1.9 %copy-done = bf16[4,384,1024]{2,1,0:T(8,128)(2,1)S(1)} copy-done((bf16[4,384,1024]{2,1,0:T(8,128)(2,1)S(1)}, bf16[4,384,1024]{2,1,0:T(8,128)(2,1)}, u32[]{:S(2)}) %copy-start) | copy-done | bytes 3145752
  111.9 0.0 copy-start.1
  111.9 1.1 copy-done.1
  112.9 0.0 copy-start.2
  112.9 0.9 copy-done.2
  113.8 0.0 copy-start.3
  113.8 0.9 copy-done.3
  114.7 6.6 %shard_map.86 = (bf16[24,2048]{1,0:T(8,128)(2,1)}, bf16[24,2048]{1,0:T(8,128)(2,1)}, bf16[768,4096]{1,0:T(8,128)(2,1)}) custom-call(bf16[768,384]{1,0:T(8,128)(2,1)S(1)} %copy-done.1, bf16[4,384,1024]{2,1,0:T(8,128)(2,1)S(1)} %copy-done, bf16[24,2048]{1,0:T(8,128)(2,1)S(1)} %copy-done.2, bf16[24,2048]{1,0:T(8,128)(2,1)S(1)} %copy-done.3), custom_call_target="tpu_custom_call" | custom-call | flops 2415919104 | bytes 12582912 | tf_op jit(solution)/shard_map/pallas_call | solution.py:651
Async XLA Ops:
  110.0 1.9 %copy-start = (bf16[4,384,1024]{2,1,0:T(8,128)(2,1)S(1)}, bf16[4,384,1024]{2,1,0:T(8,128)(2,1)}, u32[]{:S(2)}) copy-start(bf16[4,384,1024]{2,1,0:T(8,128)(2,1)} %get-tuple-element.11.scaled_ref) | copy-start | bytes 9437188
  111.9 1.1 copy-start.1
  112.9 0.9 copy-start.2
  113.8 0.9 copy-start.3
where the time goes:
time: 122 us; the launch traced here: 121 us
  Pallas kernels  113 us (93%)
  local copies, waits for them, and re-layouts  7.45 us (6%)
    pallas_call x1, Pallas kernels, dense(): pl.pallas_call(functools.partial(fused_kernel, n_z), out_shape=(jax.Shape...  107 us
    unnamed x10, local copies, waits for them, and re-layouts  7.45 us
    pallas_call x1, Pallas kernels, dense(): pl.pallas_call(last_kernel, grid=(8,), out_shape=(jax.ShapeDtypeStruct((r...  6.58 us

commit v1 on v0

--- a/solution.py
+++ b/solution.py
@@ -216,11 +216,12 @@
     for h in range(2):
         buf[expert, quarter(0, h)] = own[:, h * part : (h + 1) * part].astype(BF16)
     lanes_of = lax.broadcasted_iota(jnp.int32, (rows, 128), 1)
+    experts_of = lax.broadcasted_iota(jnp.int32, (128, rows), 0)
     named, weight = routing_ref[...], gates_ref[...]
-    table = jnp.zeros((rows, 128), F32)
-    for k in range(named.shape[1]):
-        table += jnp.where(named[:, k : k + 1] == lanes_of, weight[:, k : k + 1], 0.0)
-    tables[expert] = table
+    table = jnp.zeros((128, rows), F32)
+    for k in range(named.shape[0]):
+        table += jnp.where(named[k : k + 1] == experts_of, weight[k : k + 1], 0.0)
+    tables[expert] = table.T
     pl.semaphore_wait(barrier, len(partners))
 
     pending = []
@@ -331,23 +332,6 @@
     split_some(2)
     for j in near:
         spread(j, 1)
-    for j in rest:
-        second_a(j)
-    split_some(3)
-    for j in rest:
-        spread(j, 1)
-    for j in z_order:
-        second_b(j)
-    for j in range(n_z):
-        table_arrived(j, 1, core)
-        pass_table(j, 1, to_sib, ts_send.at[2 * j + 1])
-    for j in range(n_z):
-        for dx in range(2):
-            table_arrived(j, dx, other)
-    for e in range(2 * n_chips):
-        mine = jnp.sum(jnp.where(lanes_of == expert, tables[e], 0.0), axis=1, keepdims=True)
-        gate_ref[e * rows : (e + 1) * rows, :] = jnp.broadcast_to(mine, (rows, 128))
-
     keep_scaled = []
 
     def forward(dy, h, first):
@@ -369,7 +353,7 @@
         keep_scaled.append(copy)
         if first:
             load_out.wait()
-        tile = 256
+        tile = hidden
         deep = pl.ds(pl.multiple_of(q * part, part), part)
 
         def gates_up(n, carry):
@@ -399,8 +383,24 @@
                 arrived(j, dx, dy, h, core)
                 to_sibling(j, dx, dy, h)
 
+    for j in rest:
+        second_a(j)
+    for j in range(n_z):
+        table_arrived(j, 1, core)
+        pass_table(j, 1, to_sib, ts_send.at[2 * j + 1])
+    split_some(3)
+    for j in range(n_z):
+        for dx in range(2):
+            table_arrived(j, dx, other)
+    for e in range(2 * n_chips):
+        mine = jnp.sum(jnp.where(lanes_of == expert, tables[e], 0.0), axis=1, keepdims=True)
+        gate_ref[e * rows : (e + 1) * rows, :] = jnp.broadcast_to(mine, (rows, 128))
     from_sibling(0, 0)
     forward(0, 0, True)
+    for j in rest:
+        spread(j, 1)
+    for j in z_order:
+        second_b(j)
     third(0, 1, [1])
     from_sibling(0, 1)
     forward(0, 1, False)
@@ -426,23 +426,17 @@
 
     def backward(dy, h, part_at):
         q = quarter(dy, h)
-        tile = 256
-        steps = part // tile // 2
-
-        def step(n, carry):
-            lanes = pl.ds(pl.multiple_of(n * tile, tile), tile)
-            at = pl.ds(pl.multiple_of(q * part + n * tile, tile), tile)
-            out = jnp.dot(act[...], w_out[:, at], preferred_element_type=F32) * gate_ref[:, 0:1]
-            back = lax.dot_general(grad_both[...], w_in[at, :], NT, preferred_element_type=F32)
-            for e in range(2 * n_chips):
-                take = slice(e * rows, (e + 1) * rows)
-                parts[e % 2, q, e // 2, :, lanes] = jnp.concatenate(
-                    [out[take], back[take]], axis=0
-                ).astype(BF16)
-            return carry
-
-        lax.fori_loop(part_at * steps, (part_at + 1) * steps, step, 0)
-        lanes = pl.ds(part_at * (part // 2), part // 2)
+        tile = part // 2
+
+        lanes = pl.ds(part_at * tile, tile)
+        at = pl.ds(pl.multiple_of(q * part + part_at * tile, tile), tile)
+        out = jnp.dot(act[...], w_out[:, at], preferred_element_type=F32) * gate_ref[:, 0:1]
+        back = lax.dot_general(grad_both[...], w_in[at, :], NT, preferred_element_type=F32)
+        for e in range(2 * n_chips):
+            take = slice(e * rows, (e + 1) * rows)
+            parts[e % 2, q, e // 2, :, lanes] = jnp.concatenate(
+                [out[take], back[take]], axis=0
+            ).astype(BF16)
         sib_copies[dy, h, part_at] = send(
             parts.at[other, q, :, :, lanes],
             sib_in.at[q, :, :, lanes],
@@ -451,58 +445,72 @@
             to_sib,
         )
 
-    def chip_sum(dy, h):
+    def half(part_at):
+        return pl.ds(part_at * (part // 2), part // 2)
+
+    def chip_sum(dy, h, part_at):
         q = quarter(dy, h)
-        sib_copies[dy, h, 0].wait_recv()
-        sib_copies[dy, h, 1].wait_recv()
+        lanes = half(part_at)
+        sib_copies[dy, h, part_at].wait_recv()
 
         def add(p, carry):
-            parts[core, q, p] = (parts[core, q, p].astype(F32) + sib_in[q, p].astype(F32)).astype(BF16)
+            parts[core, q, p, :, lanes] = (
+                parts[core, q, p, :, lanes].astype(F32) + sib_in[q, p, :, lanes].astype(F32)
+            ).astype(BF16)
             return carry
 
         lax.fori_loop(0, n_chips, add, 0)
 
-    def first_a(j, dx):
-        p = chip_at(j, dx)
+    def first_a(j, dx, part_at):
+        k, lanes = j * 2 + dx, half(part_at)
         return send(
-            parts.at[core, quarter(1, 0), p],
-            one_a.at[j * 2 + dx],
-            one_send.at[j * 2 + dx],
-            one_a_recv.at[j * 2 + dx],
+            parts.at[core, quarter(1, 0), chip_at(j, dx), :, lanes],
+            one_a.at[k, :, lanes],
+            one_send.at[k, part_at],
+            one_a_recv.at[k, part_at],
             to_y,
         )
 
-    def first_b(j, dy):
-        k = j * 2 + dy
+    def first_b(j, dy, part_at):
+        k, lanes = j * 2 + dy, half(part_at)
         return send(
-            parts.at[core, quarter(dy, 1), chip_at(j, 1)],
-            one_b.at[k],
-            one_send.at[2 * n_z + k],
-            one_b_recv.at[k],
+            parts.at[core, quarter(dy, 1), chip_at(j, 1), :, lanes],
+            one_b.at[k, :, lanes],
+            one_send.at[2 * n_z + k, part_at],
+            one_b_recv.at[k, part_at],
             to_x,
         )
 
     far = [1 + k for k in range(n_z - 1)] + [0]
     a_copies, b_copies, sib_copies = {}, {}, {}
+
+    def send_a(part_at):
+        chip_sum(1, 0, part_at)
+        for dx in (1, 0):
+            for j in far:
+                a_copies[j, dx, part_at] = first_a(j, dx, part_at)
+
+    def send_b(dy, part_at):
+        chip_sum(dy, 1, part_at)
+        for j in far:
+            b_copies[j, dy, part_at] = first_b(j, dy, part_at)
+
     backward(1, 0, 0)
+    backward(1, 1, 0)
+    send_a(0)
     backward(1, 0, 1)
-    backward(1, 1, 0)
-    chip_sum(1, 0)
-    for dx in (1, 0):
-        for j in far:
-            a_copies[j, dx] = first_a(j, dx)
+    send_b(1, 0)
     backward(1, 1, 1)
+    send_a(1)
     backward(0, 1, 0)
-    chip_sum(1, 1)
-    for j in far:
-        b_copies[j, 1] = first_b(j, 1)
+    send_b(1, 1)
     backward(0, 1, 1)
+    send_b(0, 0)
     backward(0, 0, 0)
-    chip_sum(0, 1)
-    for j in far:
-        b_copies[j, 0] = first_b(j, 0)
+    send_b(0, 1)
     backward(0, 0, 1)
-    chip_sum(0, 0)
+    chip_sum(0, 0, 0)
+    chip_sum(0, 0, 1)
 
     keep_act = pltpu.make_async_copy(act_t, act_t_hbm, w_sem.at[1])
     two_copies = {}
@@ -512,7 +520,8 @@
             keep_act.start()
         p = chip_at(j, 1)
         qa, qb = quarter(0, 0), quarter(1, 1)
-        a_copies[j, 1].wait_recv()
+        for i in range(2):
+            a_copies[j, 1, i].wait_recv()
         parts[core, qa, p] = (
             parts[core, qa, p].astype(F32) + one_a[j * 2 + 1].astype(F32)
         ).astype(BF16)
@@ -520,7 +529,8 @@
             parts.at[core, qa, p], two.at[0, j], two_send.at[0, j], two_recv.at[0, j], to_x
         )
         p = chip_at(j, 0)
-        b_copies[j, 1].wait_recv()
+        for i in range(2):
+            b_copies[j, 1, i].wait_recv()
         parts[core, qb, p] = (
             parts[core, qb, p].astype(F32) + one_b[j * 2 + 1].astype(F32)
         ).astype(BF16)
@@ -534,7 +544,8 @@
             q, p = quarter(0, h), chip_at(j, 0)
             first = (a_copies, b_copies)[h]
             held = (one_a, one_b)[h]
-            first[j, 0].wait_recv()
+            for i in range(2):
+                first[j, 0, i].wait_recv()
             two_copies[j, h].wait_recv()
             total = (
                 parts[core, q, p].astype(F32)
@@ -630,9 +641,9 @@
             dma((n_experts, 4)),
             dma((4, 2)),
             dma((4, 2)),
-            dma((4 * n_z,)),
-            dma((2 * n_z,)),
-            dma((2 * n_z,)),
+            dma((4 * n_z, 2)),
+            dma((2 * n_z, 2)),
+            dma((2 * n_z, 2)),
             dma((2, n_z)),
             dma((2, n_z)),
             dma((2, n_z - 1)),
@@ -645,7 +656,7 @@
         cost_estimate=pl.CostEstimate(
             flops=flops, bytes_accessed=8 * model_width * hidden, transcendentals=slots * hidden
         ),
-    )(tokens, grad_out, routing, gates, w_in[0], w_out[0])
+    )(tokens, grad_out, routing.T, gates.T, w_in[0], w_out[0])
     tile = part // 2
     whole = pl.BlockSpec((rows, width), lambda n: (0, 0))
     mixed, gtok, gdown = pl.pallas_call(
@@ -663,7 +674,7 @@
             whole,
         ],
         out_specs=(whole, whole, pl.BlockSpec((hidden, tile), lambda n: (0, n))),
-        compiler_params=pltpu.CompilerParams(vmem_limit_bytes=32 * 1024 * 1024),
+        compiler_params=pltpu.CompilerParams(vmem_limit_bytes=60 * 1024 * 1024),
         cost_estimate=pl.CostEstimate(
             flops=flops // 7, bytes_accessed=4 * model_width * hidden, transcendentals=0
         ),

time: 122 us -> 106 us (0.87)
  Pallas kernels: 113 us -> 105 us
  local copies, waits for them, and re-layouts: 7.45 us -> 0 us
    pallas_call x1, Pallas kernels: 107 us -> 95.9 us  [dense(): pl.pallas_call(functools.partial(fused_kernel, n_z), out_shape=(jax.Shape...]
    unnamed x10 -> x0, local copies, waits for them, and re-layouts: 7.45 us -> none
    pallas_call x1, Pallas kernels: 6.58 us -> 8.99 us  [dense(): pl.pallas_call(last_kernel, grid=(8,), out_shape=(jax.ShapeDtypeStruct((r...]
where the time goes in v1:
time: 106 us
  Pallas kernels  105 us (99%)
    pallas_call x1, Pallas kernels, dense(): pl.pallas_call(functools.partial(fused_kernel, n_z), out_shape=(jax.Shape...  95.9 us
    pallas_call x1, Pallas kernels, dense(): pl.pallas_call(last_kernel, grid=(8,), out_shape=(jax.ShapeDtypeStruct((r...  8.99 us

profile of v1, /device:TPU:9, one launch (start us, length us, event | category | flops | bytes accessed | tf_op | source)
XLA Modules:
  0.0 105.6 jit_solution(2173707068673822908)
XLA Ops:
  0.6 95.9 %shard_map.85 = (bf16[24,2048]{1,0:T(8,128)(2,1)}, bf16[24,2048]{1,0:T(8,128)(2,1)}, bf16[768,384]{1,0:T(8,128)(2,1)}, bf16[4,384,1024]{2,1,0:T(8,128)(2,1)}) custom-call(bf16[24,2048]{1,0:T(8,128)(2,1)} %tok_ref.1, bf16[24,2048]{1,0:T(8,128)(2,1)} %dy_ref.1, s32[8,24]{1,0:T(8,128)} %bitcast.7, f32[8,24]{1,0:T(8,128)} %bitcast.8, ...), custom_call_target="tpu_custom_call" | custom-call | flops 16911433728 | bytes 25165824 | tf_op jit(solution)/shard_map/pallas_call | solution.py:601
  96.6 9.0 %shard_map.86 = (bf16[24,2048]{1,0:T(8,128)(2,1)}, bf16[24,2048]{1,0:T(8,128)(2,1)}, bf16[768,4096]{1,0:T(8,128)(2,1)}) custom-call(bf16[768,384]{1,0:T(8,128)(2,1)} %get-tuple-element.10.act_t_ref, bf16[4,384,1024]{2,1,0:T(8,128)(2,1)} %get-tuple-element.11.scaled_ref, bf16[24,2048]{1,0:T(8,128)(2,1)} %get-tuple-element.12.mixed_in, ...), custom_call_target="tpu_custom_call" | custom-call | flops 2415919104 | bytes 12582912 | tf_op jit(solution)/shard_map/pallas_call | solution.py:662
